TPU v7x, 32 devices: a whole 2x2x4 slice. The times are simulated.
32 devices in a mesh: group: 2 (over y), ctx: 2 (over x), exp: 8 (over z, core).
Axes of the slice: x: 2, y: 2, z: 4, core: 2. Of those that a mesh axis runs over, the one named last changes fastest.
Arguments:
- queries: bfloat16 [1024, 2048], P(('group', 'ctx'), 'exp'), parts along dimension 0, may hold values from -80 to 80
- keys: bfloat16 [1024, 2048], P(('group', 'ctx'), 'exp'), parts along dimension 0, may hold values from -4 to 4
- values: bfloat16 [1024, 2048], P(('group', 'ctx'), 'exp'), parts along dimension 0, may hold values from -6 to 6
- out_weight: bfloat16 [2048, 2048], P('exp'), may hold values from -0.125 to 0.125
- residual_in: bfloat16 [1024, 2048], P(('group', 'ctx', 'exp')), parts along dimension 0, may hold values from -6 to 6
- gate_weight: bfloat16 [8, 2048, 704], P('exp', 'ctx'), may hold values from -0.125 to 0.125
- up_weight: bfloat16 [8, 2048, 704], P('exp', 'ctx'), may hold values from -0.125 to 0.125
- down_weight: bfloat16 [8, 704, 2048], P('exp', None, 'ctx'), may hold values from -0.21875 to 0.21875
- expert_ids: int32 [1024, 2], P(('group', 'ctx', 'exp')), parts along dimension 0, may hold values from 0 to 7, all different within a row; in each aligned block of 32 rows (0 to 31, 32 to 63, ...) at most 16 rows name the same one
- route_gates: float32 [1024, 2], P(('group', 'ctx', 'exp')), parts along dimension 0, may hold values from 0.2 to 1
Outputs:
- mixed: bfloat16 [1024, 2048], P(('group', 'ctx', 'exp')), parts along dimension 0
There are 2 independent parts, one for each index of `group`. A program takes and returns all parts, laid end to end along the dimension named above; an argument that names none is the same for every part. Nothing has to cross between parts.
Inputs may be any that keep to these rules, and one draw needn't show every extreme that they name: `expert_ids`: in each aligned block of 32 rows (the rows of one device), no expert is named more than 16 times; the two experts of a row differ.
All inputs are finite; a program needn't handle non-finite values.
Results may differ from a plain program's by a relative error of at most 0.012.
Values may be sent and summed in bfloat16 or wider, within the bound.
A program may use at most 128 MiB of HBM per device.

v0:
```python
import jax
import jax.numpy as jnp
from jax import lax
from jax.sharding import PartitionSpec as P

D = 2048
HEAD_DIM = 128
CAP = 16


def per_device(
    queries,
    keys,
    values,
    out_weight,
    residual_in,
    gate_weight,
    up_weight,
    down_weight,
    expert_ids,
    route_gates,
):
    scale = HEAD_DIM ** (-0.5)
    local_tokens = queries.shape[0]
    head_count = queries.shape[1] // HEAD_DIM
    query_heads = queries.reshape(local_tokens, head_count, HEAD_DIM)
    key_piece = lax.all_gather(keys, "ctx", axis=0, tiled=True)
    value_piece = lax.all_gather(values, "ctx", axis=0, tiled=True)
    count = key_piece.shape[0]
    key_heads = key_piece.reshape(count, head_count, HEAD_DIM)
    value_heads = value_piece.reshape(count, head_count, HEAD_DIM)
    running_max = jnp.full((head_count, local_tokens), -1e30, jnp.float32)
    scores = (
        jnp.einsum("qhd,khd->hqk", query_heads, key_heads, preferred_element_type=jnp.float32)
        * scale
    )
    newest_max = jnp.maximum(running_max, jnp.max(scores, axis=2))
    weights = jnp.exp(scores - newest_max[:, :, None])
    numerator = jnp.einsum(
        "hqk,khd->hqd",
        weights.astype(jnp.bfloat16),
        value_heads,
        preferred_element_type=jnp.float32,
    )
    denominator = jnp.sum(weights, axis=2)
    final_max, numerator, denominator = (newest_max, numerator, denominator)
    attention = (numerator / denominator[:, :, None]).astype(jnp.bfloat16)
    attention = jnp.transpose(attention, (1, 0, 2)).reshape(local_tokens, head_count * HEAD_DIM)
    own_rows = residual_in.shape[0]
    hidden = residual_in.astype(jnp.float32) + lax.psum_scatter(
        jnp.dot(attention, out_weight, preferred_element_type=jnp.float32).astype(jnp.bfloat16),
        "exp",
        scatter_dimension=0,
        tiled=True,
    ).astype(jnp.float32)
    normed = (hidden * lax.rsqrt(jnp.mean(hidden * hidden, axis=1, keepdims=True) + 1e-06)).astype(
        jnp.bfloat16
    )
    owners = lax.axis_size("exp")
    flat_ids = expert_ids.reshape(-1)
    one_hot = (flat_ids[:, None] == jnp.arange(owners, dtype=jnp.int32)[None, :]).astype(jnp.int32)
    earlier = jnp.cumsum(one_hot, axis=0) - one_hot
    slot_index = jnp.sum(earlier * one_hot, axis=1)
    target = flat_ids * CAP + slot_index
    dispatch_table = (target[None, :] == jnp.arange(owners * CAP, dtype=jnp.int32)[:, None]).astype(
        jnp.bfloat16
    )
    routed = jnp.repeat(normed, 2, axis=0)
    outgoing = jnp.dot(dispatch_table, routed, preferred_element_type=jnp.float32).astype(
        jnp.bfloat16
    )
    incoming = lax.all_to_all(
        outgoing.reshape(owners, CAP, D), "exp", split_axis=0, concat_axis=0, tiled=True
    )
    slot_rows = incoming.reshape(owners * CAP, D)
    gate_part = jnp.dot(
        slot_rows,
        lax.all_gather(gate_weight[0], "ctx", axis=0, tiled=True),
        preferred_element_type=jnp.float32,
    )
    up_part = jnp.dot(
        slot_rows,
        lax.all_gather(up_weight[0], "ctx", axis=0, tiled=True),
        preferred_element_type=jnp.float32,
    )
    activation = (jax.nn.silu(gate_part) * up_part).astype(jnp.bfloat16)
    expert_result = jnp.dot(
        activation,
        lax.all_gather(down_weight[0], "ctx", axis=1, tiled=True),
        preferred_element_type=jnp.float32,
    ).astype(jnp.bfloat16)
    returned = lax.all_to_all(
        expert_result.reshape(owners, CAP, D), "exp", split_axis=0, concat_axis=0, tiled=True
    )
    per_route = jnp.einsum(
        "sr,sd->rd",
        dispatch_table,
        returned.reshape(owners * CAP, D),
        preferred_element_type=jnp.float32,
    )
    per_route = per_route.reshape(own_rows, 2, D)
    combined = per_route[:, 0, :] * route_gates[:, 0:1] + per_route[:, 1, :] * route_gates[:, 1:2]
    return (hidden + combined).astype(jnp.bfloat16)


def solution(mesh):
    return jax.shard_map(
        per_device,
        mesh=mesh,
        in_specs=(
            P(("group", "ctx"), "exp"),
            P(("group", "ctx"), "exp"),
            P(("group", "ctx"), "exp"),
            P("exp", None),
            P(("group", "ctx", "exp"), None),
            P("exp", "ctx", None),
            P("exp", "ctx", None),
            P("exp", None, "ctx"),
            P(("group", "ctx", "exp"), None),
            P(("group", "ctx", "exp"), None),
        ),
        out_specs=P(("group", "ctx", "exp"), None),
        check_vma=False,
    )
```

profile of v0, /device:TPU:3, one launch (start us, length us, event | category | flops | bytes accessed | tf_op | source)
XLA Modules:
  0.0 188.8 jit_solution(9635494611523801016)
XLA Ops:
  7.4 1.1 copy.25
  8.5 5.0 %all_gather.15 = bf16[512,256]{0,1:T(8,128)(2,1)S(1)} all-gather(bf16[256,256]{0,1:T(8,128)(2,1)S(1)} %copy.25), channel_id=1, replica_groups=mesh['group'=2,'ctx'=2,'exp'=8] {'ctx'}, dimensions={0}, use_global_device_ids=true | all-gather | bytes 393216 | tf_op jit(solution)/shard_map/all_gather | solution.py:27
  13.5 1.3 fusion.43
  14.8 4.7 %all_gather.16 = bf16[512,256]{1,0:T(8,128)(2,1)S(1)} all-gather(bf16[256,256]{1,0:T(8,128)(2,1)} %param.12), channel_id=1, replica_groups=mesh['group'=2,'ctx'=2,'exp'=8] {'ctx'}, dimensions={0}, use_global_device_ids=true | all-gather | bytes 393216 | tf_op jit(solution)/shard_map/all_gather | solution.py:28
  19.5 0.1 copy.28
  19.6 0.3 fusion.19
  20.0 0.4 fusion.16
  20.4 1.5 convolution_convert_fusion
  22.0 0.5 all-gather.7.cloned.1.call-update
  22.6 0.5 all-gather.11.cloned.1.call-update
  23.2 0.5 all-gather.9.cloned.1.call-update
  23.8 0.1 reshape.74
  24.0 0.1 reduce_window_sum.11
  24.1 0.2 select_reduce_fusion
  24.3 30.4 %reduce-scatter.2.cloned.1.call-done = bf16[32,2048]{1,0:T(8,128)(2,1)} async-done(((bf16[256,2048]{1,0:T(8,128)(2,1)}), bf16[32,2048]{1,0:T(8,128)(2,1)}) %reduce-scatter.2.cloned.1.call-update) | async-done | bytes 131088 | tf_op jit(solution)/shard_map/reduce_scatter | solution.py:50
  54.7 1.1 multiply_reduce_fusion
  55.7 1.0 multiply_convert_fusion
  56.7 0.1 broadcast_in_dim.5
  56.9 0.1 reshape.75
  57.0 1.1 convolution_convert_fusion.1
  58.1 7.1 %all-to-all-start = ((bf16[8,16,2048]{2,1,0:T(8,128)(2,1)}), bf16[8,16,2048]{2,1,0:T(8,128)(2,1)S(1)}, u32[]{:S(2)}, u32[]{:S(2)}) async-start(bf16[8,16,2048]{2,1,0:T(8,128)(2,1)} %bitcast.6), calls=%async_computation.1 | async-start | bytes 1048576 | tf_op jit(solution)/shard_map/all_to_all | solution.py:72
  65.2 2.9 %all-gather.7.cloned.1.call-done = bf16[1,2048,704]{1,2,0:T(8,128)(2,1)} async-done(((bf16[1,1024,704]{1,2,0:T(8,128)(2,1)}), bf16[1,2048,704]{1,2,0:T(8,128)(2,1)}) %all-gather.7.cloned.1.call-update) | async-done | bytes 2883600 | tf_op jit(solution)/shard_map/all_gather | solution.py:78
  68.1 11.6 %all-to-all-done = bf16[8,16,2048]{2,1,0:T(8,128)(2,1)S(1)} async-done(((bf16[8,16,2048]{2,1,0:T(8,128)(2,1)}), bf16[8,16,2048]{2,1,0:T(8,128)(2,1)S(1)}, u32[]{:S(2)}, u32[]{:S(2)}) %all-to-all-start) | async-done | bytes 524320 | tf_op jit(solution)/shard_map/all_to_all | solution.py:72
  79.7 2.9 %fusion.4 = f32[128,704]{0,1:T(8,128)S(1)} fusion(bf16[128,2048]{1,0:T(8,128)(2,1)S(1)} %bitcast.73, bf16[1,2048,704]{1,2,0:T(8,128)(2,1)} %all-gather.7.cloned.1.call-done), kind=kOutput, calls=%fused_computation.4 | convolution fusion | flops 369098752 | bytes 3768320 | tf_op jit(solution)/shard_map/dot_general | solution.py:76
  82.7 28.6 %all-gather.11.cloned.1.call-done = bf16[1,704,2048]{2,1,0:T(8,128)(2,1)} async-done(((bf16[1,704,1024]{2,1,0:T(8,128)(2,1)}), bf16[1,704,2048]{2,1,0:T(8,128)(2,1)}) %all-gather.11.cloned.1.call-update) | async-done | bytes 2883600 | tf_op jit(solution)/shard_map/all_gather | solution.py:89
  111.4 43.3 %all-gather.9.cloned.1.call-done = bf16[1,2048,704]{1,2,0:T(8,128)(2,1)} async-done(((bf16[1,1024,704]{1,2,0:T(8,128)(2,1)}), bf16[1,2048,704]{1,2,0:T(8,128)(2,1)}) %all-gather.9.cloned.1.call-update) | async-done | bytes 2883600 | tf_op jit(solution)/shard_map/all_gather | solution.py:83
  154.6 5.6 %fusion.6 = bf16[128,2048]{1,0:T(8,128)(2,1)} fusion(bf16[1,704,2048]{2,1,0:T(8,128)(2,1)} %all-gather.11.cloned.1.call-done, bf16[128,2048]{1,0:T(8,128)(2,1)S(1)} %bitcast.74, bf16[1,2048,704]{1,2,0:T(8,128)(2,1)} %all-gather.9.cloned.1.call-done, f32[128,704]{0,1:T(8,128)S(1)} %fusion.4), kind=kOutput, calls=%fused_computation.7 | convolution fusion | flops 739000320 | bytes 7176192 | tf_op jit(solution)/shard_map/dot_general | solution.py:87
  160.2 5.4 %all-to-all-start.1 = ((bf16[8,16,2048]{2,1,0:T(8,128)(2,1)}), bf16[8,16,2048]{2,1,0:T(8,128)(2,1)S(1)}, u32[]{:S(2)}, u32[]{:S(2)}) async-start(bf16[8,16,2048]{2,1,0:T(8,128)(2,1)} %bitcast.11), calls=%async_computation.2 | async-start | bytes 1048576 | tf_op jit(solution)/shard_map/all_to_all | solution.py:92
  165.6 0.1 reduce_sum.31
  165.8 14.3 %all-to-all-done.1 = bf16[8,16,2048]{2,1,0:T(8,128)(2,1)S(1)} async-done(((bf16[8,16,2048]{2,1,0:T(8,128)(2,1)}), bf16[8,16,2048]{2,1,0:T(8,128)(2,1)S(1)}, u32[]{:S(2)}, u32[]{:S(2)}) %all-to-all-start.1) | async-done | bytes 524320 | tf_op jit(solution)/shard_map/all_to_all | solution.py:92
  180.1 0.3 fusion.39
  180.4 0.8 fusion.31
  (23 shorter events, 0.4 us)
Async XLA Ops:
  7.4 13.0 %copy-start = (bf16[256,2048]{1,0:T(8,128)(2,1)S(1)}, bf16[256,2048]{1,0:T(8,128)(2,1)}, u32[]{:S(2)}) copy-start(bf16[256,2048]{1,0:T(8,128)(2,1)} %param.13) | copy-start | bytes 3145732
  7.4 47.3 %reduce-scatter.2.cloned.1.call-start = ((), (), s32[]{:S(2)}) async-start(), calls=%async_computation.3 | async-start | bytes 1179648 | tf_op jit(solution)/shard_map/reduce_scatter | solution.py:50
  22.0 1.8 copy-start.3
  22.0 32.7 %copy-start.1 = (bf16[32,2048]{1,0:T(8,128)(2,1)S(1)}, bf16[32,2048]{1,0:T(8,128)(2,1)}, u32[]{:S(2)}) copy-start(bf16[32,2048]{1,0:T(8,128)(2,1)} %param.14) | copy-start | bytes 393220
  22.0 46.1 %all-gather.7.cloned.1.call-start = ((), (), s32[]{:S(2)}) async-start(), calls=%async_computation.4 | async-start | bytes 4325376 | tf_op jit(solution)/shard_map/all_gather | solution.py:78
  22.6 88.8 %all-gather.11.cloned.1.call-start = ((), (), s32[]{:S(2)}) async-start(), calls=%async_computation.6 | async-start | bytes 4325376 | tf_op jit(solution)/shard_map/all_gather | solution.py:89
  23.1 131.5 %all-gather.9.cloned.1.call-start = ((), (), s32[]{:S(2)}) async-start(), calls=%async_computation.5 | async-start | bytes 4325376 | tf_op jit(solution)/shard_map/all_gather | solution.py:83
  58.1 21.6 %all-to-all-start = ((bf16[8,16,2048]{2,1,0:T(8,128)(2,1)}), bf16[8,16,2048]{2,1,0:T(8,128)(2,1)S(1)}, u32[]{:S(2)}, u32[]{:S(2)}) async-start(bf16[8,16,2048]{2,1,0:T(8,128)(2,1)} %bitcast.6), calls=%async_computation.1 | async-start | bytes 1048576 | tf_op jit(solution)/shard_map/all_to_all | solution.py:72
  82.7 83.1 %copy-start.4 = (f32[32,2]{0,1:T(2,128)S(1)}, f32[32,2]{0,1:T(2,128)}, u32[]{:S(2)}) copy-start(f32[32,2]{0,1:T(2,128)} %param.19) | copy-start | bytes 772
  82.7 97.7 %copy-start.2 = (bf16[32,2048]{1,0:T(8,128)(2,1)S(1)}, bf16[32,2048]{1,0:T(8,128)(2,1)}, u32[]{:S(2)}) copy-start(bf16[32,2048]{1,0:T(8,128)(2,1)} %reduce-scatter.2.cloned.1.call-done) | copy-start | bytes 393220
  160.2 19.9 %all-to-all-start.1 = ((bf16[8,16,2048]{2,1,0:T(8,128)(2,1)}), bf16[8,16,2048]{2,1,0:T(8,128)(2,1)S(1)}, u32[]{:S(2)}, u32[]{:S(2)}) async-start(bf16[8,16,2048]{2,1,0:T(8,128)(2,1)} %bitcast.11), calls=%async_computation.2 | async-start | bytes 1048576 | tf_op jit(solution)/shard_map/all_to_all | solution.py:92
Sparse Core Ops, SparseCore 0:
  22.1 32.5 reduce-scatter.1
Sparse Core Ops, SparseCore 1:
  24.0 44.0 all-gather.6
  69.5 41.8 all-gather.10
  112.8 41.8 all-gather.8
where the time goes:
time: 192 us; the launch traced here: 189 us
  waiting for transfers between devices  133 us (69%)
  between operations  15.1 us (8%)
  matrix products  13.2 us (7%)
  starting transfers between devices  12.6 us (7%)
  blocking collectives  9.75 us (5%)
  other arithmetic  3.52 us (2%)
    all_gather x1, waiting for transfers between devices, per_device(): lax.all_gather(up_weight[0], 'ctx', axis=0, tiled=True)  43.3 us
    reduce_scatter x1, waiting for transfers between devices, per_device(): lax.psum_scatter(jnp.dot(attention, out_weight, preferred_element_type=jn...  30.4 us
    all_gather x1, waiting for transfers between devices, per_device(): lax.all_gather(down_weight[0], 'ctx', axis=1, tiled=True)  28.6 us
    all_to_all x1, waiting for transfers between devices, per_device(): lax.all_to_all(expert_result.reshape(owners, CAP, D), 'exp', split_axis=0...  14.3 us
    all_to_all x1, waiting for transfers between devices, per_device(): lax.all_to_all(outgoing.reshape(owners, CAP, D), 'exp', split_axis=0, con...  11.6 us
    all_to_all x1, starting transfers between devices, per_device(): lax.all_to_all(outgoing.reshape(owners, CAP, D), 'exp', split_axis=0, con...  7.09 us
    dot_general x1, matrix products, per_device(): jnp.dot(activation, lax.all_gather(down_weight[0], 'ctx', axis=1, tiled=T...  5.62 us
    all_to_all x1, starting transfers between devices, per_device(): lax.all_to_all(expert_result.reshape(owners, CAP, D), 'exp', split_axis=0...  5.39 us
  transfers between devices with their start and end apart: 6, of which 6 were waited for; matrix products, arithmetic and copies ran while one was open for 4% of the time, Pallas kernels for 0%

commit v1 on v0

--- a/solution.py
+++ b/solution.py
@@ -103,9 +103,119 @@
     return (hidden + combined).astype(jnp.bfloat16)
 
 
+def per_device_pair(
+    queries,
+    keys,
+    values,
+    out_weight,
+    residual_in,
+    gate_weight,
+    up_weight,
+    down_weight,
+    expert_ids,
+    route_gates,
+):
+    scale = HEAD_DIM ** (-0.5)
+    local_tokens = queries.shape[0]
+    head_count = queries.shape[1] // HEAD_DIM
+    swap = [(0, 1), (1, 0)]
+    me = lax.axis_index("ctx")
+    key_other = lax.ppermute(keys, "ctx", swap)
+    value_other = lax.ppermute(values, "ctx", swap)
+    query_heads = queries.reshape(local_tokens, head_count, HEAD_DIM)
+    key_heads = jnp.concatenate([keys, key_other], 0).reshape(-1, head_count, HEAD_DIM)
+    value_heads = jnp.concatenate([values, value_other], 0).reshape(-1, head_count, HEAD_DIM)
+    scores = (
+        jnp.einsum("qhd,khd->hqk", query_heads, key_heads, preferred_element_type=jnp.float32)
+        * scale
+    )
+    weights = jnp.exp(scores - jnp.max(scores, axis=2, keepdims=True))
+    numerator = jnp.einsum(
+        "hqk,khd->hqd",
+        weights.astype(jnp.bfloat16),
+        value_heads,
+        preferred_element_type=jnp.float32,
+    )
+    attention = (numerator / jnp.sum(weights, axis=2, keepdims=True)).astype(jnp.bfloat16)
+    attention = jnp.transpose(attention, (1, 0, 2)).reshape(local_tokens, head_count * HEAD_DIM)
+    own_rows = residual_in.shape[0]
+    hidden = residual_in.astype(jnp.float32) + lax.psum_scatter(
+        jnp.dot(attention, out_weight, preferred_element_type=jnp.float32).astype(jnp.bfloat16),
+        "exp",
+        scatter_dimension=0,
+        tiled=True,
+    ).astype(jnp.float32)
+    normed = (hidden * lax.rsqrt(jnp.mean(hidden * hidden, axis=1, keepdims=True) + 1e-06)).astype(
+        jnp.bfloat16
+    )
+    owners = lax.axis_size("exp")
+    slots = owners * CAP
+    half = D // 2
+    flat_ids = expert_ids.reshape(-1)
+    one_hot = (flat_ids[:, None] == jnp.arange(owners, dtype=jnp.int32)[None, :]).astype(jnp.int32)
+    earlier = jnp.cumsum(one_hot, axis=0) - one_hot
+    target = flat_ids * CAP + jnp.sum(earlier * one_hot, axis=1)
+    dispatch_table = (target[None, :] == jnp.arange(slots, dtype=jnp.int32)[:, None]).astype(
+        jnp.bfloat16
+    )
+    routed = jnp.repeat(normed, 2, axis=0)
+    halves = [
+        jnp.dot(
+            dispatch_table, routed[:, c * half : (c + 1) * half], preferred_element_type=jnp.float32
+        ).astype(jnp.bfloat16)
+        for c in range(2)
+    ]
+    incoming = lax.all_to_all(
+        jnp.concatenate(halves, 0).reshape(2 * owners, CAP, half),
+        ("ctx", "exp"),
+        split_axis=0,
+        concat_axis=0,
+        tiled=True,
+    )
+    slot_rows = incoming.reshape(2 * slots, half)
+    part = jnp.concatenate(
+        [
+            jnp.dot(slot_rows, gate_weight[0], preferred_element_type=jnp.float32),
+            jnp.dot(slot_rows, up_weight[0], preferred_element_type=jnp.float32),
+        ],
+        1,
+    )
+    mine = lax.dynamic_slice_in_dim(part, me * slots, slots, 0)
+    theirs = lax.dynamic_slice_in_dim(part, (1 - me) * slots, slots, 0)
+    whole = mine + lax.ppermute(theirs.astype(jnp.bfloat16), "ctx", swap).astype(jnp.float32)
+    hidden_units = gate_weight.shape[2]
+    activation = (jax.nn.silu(whole[:, :hidden_units]) * whole[:, hidden_units:]).astype(
+        jnp.bfloat16
+    )
+    other = lax.ppermute(activation, "ctx", swap)
+    first = jnp.where(me == 0, activation, other)
+    second = jnp.where(me == 0, other, activation)
+    expert_result = jnp.dot(
+        jnp.concatenate([first, second], 0), down_weight[0], preferred_element_type=jnp.float32
+    ).astype(jnp.bfloat16)
+    returned = lax.all_to_all(
+        expert_result.reshape(2 * owners, CAP, half),
+        ("ctx", "exp"),
+        split_axis=0,
+        concat_axis=0,
+        tiled=True,
+    ).reshape(2, slots, half)
+    per_route = jnp.concatenate(
+        [
+            jnp.einsum(
+                "sr,sd->rd", dispatch_table, returned[c], preferred_element_type=jnp.float32
+            )
+            for c in range(2)
+        ],
+        1,
+    ).reshape(own_rows, 2, D)
+    combined = per_route[:, 0, :] * route_gates[:, 0:1] + per_route[:, 1, :] * route_gates[:, 1:2]
+    return (hidden + combined).astype(jnp.bfloat16)
+
+
 def solution(mesh):
     return jax.shard_map(
-        per_device,
+        per_device_pair if mesh.shape["ctx"] == 2 else per_device,
         mesh=mesh,
         in_specs=(
             P(("group", "ctx"), "exp"),

time: 192 us -> 126 us (0.66); the launches traced: 189 us -> 125 us
  waiting for transfers between devices: 133 us -> 78.2 us
  blocking collectives: 9.75 us -> 0 us
  matrix products: 13.2 us -> 8.25 us
  other arithmetic: 3.52 us -> 6.61 us
  local copies, waits for them, and re-layouts: 1.86 us -> 4.22 us
    all_gather x3 -> x0, waiting for transfers between devices: 74.8 us -> none  [the longest x1 43.3 us: per_device(): lax.all_gather(up_weight[0], 'ctx', axis=0, tiled=True)]
    ppermute x0 -> x4, waiting for transfers between devices: none -> 18.9 us  [the longest x1 9.86 us: per_device_pair(): lax.ppermute(theirs.astype(jnp.bfloat16), 'ctx', swap).astype(jnp.float32)]
    all_gather x2 -> x0, blocking collectives: 9.75 us -> none  [the longest x1 5.04 us: per_device(): key_piece = lax.all_gather(keys, 'ctx', axis=0, tiled=True)]
    dot_general x7 -> x10, matrix products: 13.2 us -> 8.25 us  [the longest x1 1.94 us: per_device_pair(): jnp.dot(slot_rows, gate_weight[0], preferred_element_type=jnp.float32)]
    all_to_all x2, waiting for transfers between devices: 25.9 us -> 28.3 us  [the longest x1 14.1 us: per_device_pair(): lax.all_to_all(jnp.concatenate(halves, 0).reshape(2 * owners, CAP, half),...]
  transfers between devices with their start and end apart: 6 -> 7, of which waited for: 6 -> 7; matrix products, arithmetic and copies ran while one was open for 4% -> 2% of each run, Pallas kernels for 0% -> 0%
where the time goes in v1:
time: 126 us; the launch traced here: 125 us
  waiting for transfers between devices  78.2 us (62%)
  starting transfers between devices  14.1 us (11%)
  between operations  13.6 us (11%)
  matrix products  8.25 us (7%)
  other arithmetic  6.61 us (5%)
  local copies, waits for them, and re-layouts  4.22 us (3%)
    reduce_scatter x1, waiting for transfers between devices, per_device_pair(): lax.psum_scatter(jnp.dot(attention, out_weight, preferred_element_type=jn...  31 us
    all_to_all x1, waiting for transfers between devices, per_device_pair(): lax.all_to_all(jnp.concatenate(halves, 0).reshape(2 * owners, CAP, half),...  14.1 us
    all_to_all x1, waiting for transfers between devices, per_device_pair(): lax.all_to_all(expert_result.reshape(2 * owners, CAP, half), ('ctx', 'exp...  14.1 us
    ppermute x1, waiting for transfers between devices, per_device_pair(): lax.ppermute(theirs.astype(jnp.bfloat16), 'ctx', swap).astype(jnp.float32)  9.86 us
    all_to_all x1, starting transfers between devices, per_device_pair(): lax.all_to_all(jnp.concatenate(halves, 0).reshape(2 * owners, CAP, half),...  7.28 us
    ppermute x1, waiting for transfers between devices, per_device_pair(): other = lax.ppermute(activation, 'ctx', swap)  5.28 us
    all_to_all x1, starting transfers between devices, per_device_pair(): lax.all_to_all(expert_result.reshape(2 * owners, CAP, half), ('ctx', 'exp...  5.01 us
    unnamed x18, local copies, waits for them, and re-layouts  2.97 us
  transfers between devices with their start and end apart: 7, of which 7 were waited for; matrix products, arithmetic and copies ran while one was open for 2% of the time, Pallas kernels for 0%

profile of v1, /device:TPU:3, one launch (start us, length us, event | category | flops | bytes accessed | tf_op | source)
XLA Modules:
  0.0 125.1 jit_solution(12452301827906697436)
XLA Ops:
  6.6 1.1 copy.16
  7.7 1.4 %collective-permute-start = (bf16[256,256]{0,1:T(8,128)(2,1)S(1)}, bf16[256,256]{0,1:T(8,128)(2,1)S(1)}, u32[]{:S(2)}, u32[]{:S(2)}) collective-permute-start(bf16[256,256]{0,1:T(8,128)(2,1)S(1)} %copy.16), channel_id=1, source_target_pairs={{0,8},{8,0},{1,9},{9,1},{2,10},{10,2},{3,11},{11,3},{4,12},{12,4},... | collective-permute-start | bytes 393224 | tf_op jit(solution)/shard_map/ppermute | solution.py:123
  9.1 2.0 %collective-permute-done.1 = bf16[256,256]{1,0:T(8,128)(2,1)S(1)} collective-permute-done((bf16[256,256]{1,0:T(8,128)(2,1)}, bf16[256,256]{1,0:T(8,128)(2,1)S(1)}, u32[]{:S(2)}, u32[]{:S(2)}) %collective-permute-start.1) | collective-permute-done | bytes 131104 | tf_op jit(solution)/shard_map/ppermute | solution.py:124
  11.1 0.9 pad_maximum_fusion.2
  12.2 1.7 %collective-permute-done = bf16[256,256]{0,1:T(8,128)(2,1)S(1)} collective-permute-done((bf16[256,256]{0,1:T(8,128)(2,1)S(1)}, bf16[256,256]{0,1:T(8,128)(2,1)S(1)}, u32[]{:S(2)}, u32[]{:S(2)}) %collective-permute-start) | collective-permute-done | bytes 131104 | tf_op jit(solution)/shard_map/ppermute | solution.py:123
  14.0 0.4 fusion.43
  14.5 0.3 fusion.11
  14.8 0.7 copy-done.4
  15.5 1.4 %convolution_convert_fusion = bf16[256,2048]{1,0:T(8,128)(2,1)} fusion(bf16[256,256]{0,1:T(8,128)(2,1)S(1)} %bitcast.71, bf16[256,2048]{1,0:T(8,128)(2,1)S(1)} %copy-done.4), kind=kOutput, calls=%fused_computation | convolution fusion | flops 268959744 | bytes 2228224 | tf_op jit(solution)/shard_map/dot_general | solution.py:143
  17.6 31.0 %reduce-scatter.2.cloned.1.call-done = bf16[32,2048]{1,0:T(8,128)(2,1)} async-done(((bf16[256,2048]{1,0:T(8,128)(2,1)}), bf16[32,2048]{1,0:T(8,128)(2,1)}) %reduce-scatter.2.cloned.1.call-update) | async-done | bytes 131088 | tf_op jit(solution)/shard_map/reduce_scatter | solution.py:142
  48.6 1.1 multiply_reduce_fusion
  49.7 1.0 multiply_convert_fusion
  50.9 0.2 convolution_convert_fusion.2
  51.2 0.2 convolution_convert_fusion.1
  51.4 0.8 pad_maximum_fusion
  52.2 7.3 %all-to-all-start = ((bf16[16,16,1024]{2,1,0:T(8,128)(2,1)}), bf16[16,16,1024]{2,1,0:T(8,128)(2,1)S(1)}, u32[]{:S(2)}, u32[]{:S(2)}) async-start(bf16[16,16,1024]{2,1,0:T(8,128)(2,1)} %bitcast.6), calls=%async_computation.1 | async-start | bytes 1048576 | tf_op jit(solution)/shard_map/all_to_all | solution.py:168
  59.5 14.1 %all-to-all-done = bf16[16,16,1024]{2,1,0:T(8,128)(2,1)S(1)} async-done(((bf16[16,16,1024]{2,1,0:T(8,128)(2,1)}), bf16[16,16,1024]{2,1,0:T(8,128)(2,1)S(1)}, u32[]{:S(2)}, u32[]{:S(2)}) %all-to-all-start) | async-done | bytes 524320 | tf_op jit(solution)/shard_map/all_to_all | solution.py:168
  73.6 1.9 %fusion.2 = f32[256,704]{0,1:T(8,128)S(1)} fusion(bf16[256,1024]{1,0:T(8,128)(2,1)S(1)} %bitcast.65, bf16[1,1024,704]{1,2,0:T(8,128)(2,1)} %param.16), kind=kOutput, calls=%fused_computation.7 | convolution fusion | flops 369098752 | bytes 2686976 | tf_op jit(solution)/shard_map/dot_general | solution.py:179
  75.6 1.9 %fusion.4 = f32[256,704]{0,1:T(8,128)S(1)} fusion(bf16[256,1024]{1,0:T(8,128)(2,1)S(1)} %bitcast.66, bf16[1,1024,704]{1,2,0:T(8,128)(2,1)} %param.15), kind=kOutput, calls=%fused_computation.9 | convolution fusion | flops 369098752 | bytes 2686976 | tf_op jit(solution)/shard_map/dot_general | solution.py:178
  77.5 0.9 copy-done.1
  78.4 0.3 collective-permute-start.2
  78.8 9.9 %collective-permute-done.2 = bf16[128,1408]{0,1:T(8,128)(2,1)S(1)} collective-permute-done((bf16[128,1408]{0,1:T(8,128)(2,1)S(1)}, bf16[128,1408]{0,1:T(8,128)(2,1)S(1)}, u32[]{:S(2)}, u32[]{:S(2)}) %collective-permute-start.2) | collective-permute-done | bytes 360480 | tf_op jit(solution)/shard_map/ppermute | solution.py:185
  88.6 1.1 fusion.17
  89.9 5.3 %collective-permute-done.3 = bf16[128,704]{0,1:T(8,128)(2,1)S(1)} collective-permute-done((bf16[128,704]{0,1:T(8,128)(2,1)S(1)}, bf16[128,704]{0,1:T(8,128)(2,1)S(1)}, u32[]{:S(2)}, u32[]{:S(2)}) %collective-permute-start.3) | collective-permute-done | bytes 180256 | tf_op jit(solution)/shard_map/ppermute | solution.py:190
  95.4 1.4 %fusion.7 = bf16[256,1024]{1,0:T(8,128)(2,1)} fusion(bf16[1,704,1024]{2,1,0:T(8,128)(2,1)S(1)} %copy-done, bf16[128,704]{0,1:T(8,128)(2,1)S(1)} %get-tuple-element.10, bf16[128,704]{0,1:T(8,128)(2,1)S(1)} %get-tuple-element.9), kind=kOutput, calls=%fused_computation.13 | convolution fusion | flops 370081792 | bytes 2326528 | tf_op jit(solution)/shard_map/dot_general | solution.py:193
  96.8 5.0 %all-to-all-start.1 = ((bf16[16,16,1024]{2,1,0:T(8,128)(2,1)}), bf16[16,16,1024]{2,1,0:T(8,128)(2,1)S(1)}, u32[]{:S(2)}, u32[]{:S(2)}) async-start(bf16[16,16,1024]{2,1,0:T(8,128)(2,1)} %bitcast.11), calls=%async_computation.2 | async-start | bytes 1048576 | tf_op jit(solution)/shard_map/all_to_all | solution.py:196
  101.8 14.1 %all-to-all-done.1 = bf16[16,16,1024]{2,1,0:T(8,128)(2,1)S(1)} async-done(((bf16[16,16,1024]{2,1,0:T(8,128)(2,1)}), bf16[16,16,1024]{2,1,0:T(8,128)(2,1)S(1)}, u32[]{:S(2)}, u32[]{:S(2)}) %all-to-all-start.1) | async-done | bytes 524320 | tf_op jit(solution)/shard_map/all_to_all | solution.py:196
  116.0 0.2 fusion.34
  116.2 0.2 fusion.33
  116.5 0.3 reshape.63
  116.8 0.4 fusion.41
  117.4 0.9 fusion.27
  (36 shorter events, 1.8 us)
Async XLA Ops:
  6.5 88.9 %copy-start = (bf16[1,704,1024]{2,1,0:T(8,128)(2,1)S(1)}, bf16[1,704,1024]{2,1,0:T(8,128)(2,1)}, u32[]{:S(2)}) copy-start(bf16[1,704,1024]{2,1,0:T(8,128)(2,1)} %param.17) | copy-start | bytes 4325380
  6.5 7.4 %copy-start.5 = (bf16[256,256]{1,0:T(8,128)(2,1)S(1)}, bf16[256,256]{1,0:T(8,128)(2,1)}, u32[]{:S(2)}) copy-start(bf16[256,256]{1,0:T(8,128)(2,1)} %param.10) | copy-start | bytes 393220
  6.5 42.1 %reduce-scatter.2.cloned.1.call-start = ((), (), s32[]{:S(2)}) async-start(), calls=%async_computation.3 | async-start | bytes 1179648 | tf_op jit(solution)/shard_map/reduce_scatter | solution.py:142
  6.5 4.6 %collective-permute-start.1 = (bf16[256,256]{1,0:T(8,128)(2,1)}, bf16[256,256]{1,0:T(8,128)(2,1)S(1)}, u32[]{:S(2)}, u32[]{:S(2)}) collective-permute-start(bf16[256,256]{1,0:T(8,128)(2,1)} %param.12), channel_id=1, source_target_pairs={{0,8},{8,0},{1,9},{9,1},{2,10},{10,2},{3,11},{11,3},{4,12},{12,4},... | collective-permute-start | bytes 393224 | tf_op jit(solution)/shard_map/ppermute | solution.py:124
  7.7 6.2 %collective-permute-start = (bf16[256,256]{0,1:T(8,128)(2,1)S(1)}, bf16[256,256]{0,1:T(8,128)(2,1)S(1)}, u32[]{:S(2)}, u32[]{:S(2)}) collective-permute-start(bf16[256,256]{0,1:T(8,128)(2,1)S(1)} %copy.16), channel_id=1, source_target_pairs={{0,8},{8,0},{1,9},{9,1},{2,10},{10,2},{3,11},{11,3},{4,12},{12,4},... | collective-permute-start | bytes 393224 | tf_op jit(solution)/shard_map/ppermute | solution.py:123
  14.3 1.2 copy-start.4
  15.5 1.5 %copy-start.6 = (s32[32,2]{0,1:T(2,128)S(1)}, s32[32,2]{0,1:T(2,128)}, u32[]{:S(2)}) copy-start(s32[32,2]{0,1:T(2,128)} %param.18) | copy-start | bytes 772
  15.5 33.1 %copy-start.2 = (bf16[32,2048]{1,0:T(8,128)(2,1)S(1)}, bf16[32,2048]{1,0:T(8,128)(2,1)}, u32[]{:S(2)}) copy-start(bf16[32,2048]{1,0:T(8,128)(2,1)} %param.14) | copy-start | bytes 393220
  52.2 21.4 %all-to-all-start = ((bf16[16,16,1024]{2,1,0:T(8,128)(2,1)}), bf16[16,16,1024]{2,1,0:T(8,128)(2,1)S(1)}, u32[]{:S(2)}, u32[]{:S(2)}) async-start(bf16[16,16,1024]{2,1,0:T(8,128)(2,1)} %bitcast.6), calls=%async_computation.1 | async-start | bytes 1048576 | tf_op jit(solution)/shard_map/all_to_all | solution.py:168
  77.5 0.9 copy-start.1
  78.4 10.2 %collective-permute-start.2 = (bf16[128,1408]{0,1:T(8,128)(2,1)S(1)}, bf16[128,1408]{0,1:T(8,128)(2,1)S(1)}, u32[]{:S(2)}, u32[]{:S(2)}) collective-permute-start(bf16[128,1408]{0,1:T(8,128)(2,1)S(1)} %fusion.15), channel_id=1, source_target_pairs={{0,8},{8,0},{1,9},{9,1},{2,10},{10,2},{3,11},{11,3},{4,12},{12,4},... | collective-permute-start | bytes 1081352 | tf_op jit(solution)/shard_map/ppermute | solution.py:185
  89.8 5.4 %collective-permute-start.3 = (bf16[128,704]{0,1:T(8,128)(2,1)S(1)}, bf16[128,704]{0,1:T(8,128)(2,1)S(1)}, u32[]{:S(2)}, u32[]{:S(2)}) collective-permute-start(bf16[128,704]{0,1:T(8,128)(2,1)S(1)} %fusion.20), channel_id=1, source_target_pairs={{0,8},{8,0},{1,9},{9,1},{2,10},{10,2},{3,11},{11,3},{4,12},{12,4},... | collective-permute-start | bytes 540680 | tf_op jit(solution)/shard_map/ppermute | solution.py:190
  95.4 6.4 %copy-start.7 = (f32[32,2]{0,1:T(2,128)S(1)}, f32[32,2]{0,1:T(2,128)}, u32[]{:S(2)}) copy-start(f32[32,2]{0,1:T(2,128)} %param.19) | copy-start | bytes 772
  96.8 19.2 %all-to-all-start.1 = ((bf16[16,16,1024]{2,1,0:T(8,128)(2,1)}), bf16[16,16,1024]{2,1,0:T(8,128)(2,1)S(1)}, u32[]{:S(2)}, u32[]{:S(2)}) async-start(bf16[16,16,1024]{2,1,0:T(8,128)(2,1)} %bitcast.11), calls=%async_computation.2 | async-start | bytes 1048576 | tf_op jit(solution)/shard_map/all_to_all | solution.py:196
  116.5 0.9 copy-start.3
Sparse Core Ops, SparseCore 0:
  17.1 31.4 reduce-scatter.1

commit v2 on v0

--- a/solution.py
+++ b/solution.py
@@ -1,6 +1,10 @@
+import functools
+
 import jax
 import jax.numpy as jnp
 from jax import lax
+from jax.experimental import pallas as pl
+from jax.experimental.pallas import tpu as pltpu
 from jax.sharding import PartitionSpec as P
 
 D = 2048
@@ -103,9 +107,370 @@
     return (hidden + combined).astype(jnp.bfloat16)
 
 
+F32 = jnp.float32
+BF16 = jnp.bfloat16
+HALF = D // 2
+
+
+def dot(a, b):
+    return jnp.dot(a, b, preferred_element_type=F32)
+
+
+def block_kernel(
+    owners,
+    q_ref,
+    k_ref,
+    v_ref,
+    wo_hbm,
+    res_ref,
+    wg_hbm,
+    wu_hbm,
+    wd_hbm,
+    ids_ref,
+    gates_ref,
+    out_ref,
+    wo,
+    wg,
+    wu,
+    wd,
+    k_other,
+    v_other,
+    q_sorted,
+    attn,
+    mate_out,
+    mate_in,
+    own_part,
+    reduce_out,
+    reduce_in,
+    hidden,
+    outgoing,
+    slab,
+    part_out,
+    part_in,
+    act_own,
+    act_other,
+    results,
+    returned,
+    load_sem,
+    kv_send,
+    kv_recv,
+    mate_send,
+    mate_recv,
+    red_send,
+    red_recv,
+    disp_send,
+    disp_recv,
+    part_send,
+    part_recv,
+    act_send,
+    act_recv,
+    ret_send,
+    ret_recv,
+):
+    chips = owners // 2
+    ctx = lax.axis_index("ctx")
+    exp = lax.axis_index("exp")
+    chip, core = exp // 2, lax.rem(exp, 2)
+    rows = res_ref.shape[0]
+    slots = owners * CAP
+    group_rows = chips * rows
+    other_ctx = 1 - ctx
+
+    def place(dc, de):
+        return {
+            "ctx": other_ctx if dc else ctx,
+            "exp": lax.rem(exp + de, owners) if de else exp,
+        }
+
+    def remote(src, dst, send, recv, where):
+        copy = pltpu.make_async_remote_copy(
+            src_ref=src,
+            dst_ref=dst,
+            send_sem=send,
+            recv_sem=recv,
+            device_id=where,
+            device_id_type=pl.DeviceIdType.MESH,
+        )
+        copy.start()
+        return copy
+
+    loads = []
+    for n, (src, dst) in enumerate(((wo_hbm, wo), (wg_hbm, wg), (wu_hbm, wu), (wd_hbm, wd))):
+        load = pltpu.make_async_copy(src, dst, load_sem.at[n])
+        load.start()
+        loads.append(load)
+
+    partners = [(dc, de) for dc in range(2) for de in range(owners) if dc or de]
+    barrier = pltpu.get_barrier_semaphore()
+    for dc, de in partners:
+        pl.semaphore_signal(
+            barrier, inc=1, device_id=place(dc, de), device_id_type=pl.DeviceIdType.MESH
+        )
+    pl.semaphore_wait(barrier, len(partners))
+
+    across = place(1, 0)
+    k_copy = remote(k_ref, k_other, kv_send.at[0], kv_recv.at[0], across)
+    v_copy = remote(v_ref, v_other, kv_send.at[1], kv_recv.at[1], across)
+
+    lane = lax.broadcasted_iota(jnp.int32, (rows, slots), 1)
+    picks = []
+    for k in range(2):
+        rel = ids_ref[:, k : k + 1] - exp
+        picks.append(jnp.where(rel < 0, rel + owners, rel))
+    named = [jnp.where(lane == rel, 1.0, 0.0) for rel in picks]
+    below = jnp.where(
+        lax.broadcasted_iota(jnp.int32, (rows, rows), 0)
+        > lax.broadcasted_iota(jnp.int32, (rows, rows), 1),
+        1.0,
+        0.0,
+    )
+    earlier = dot(below.astype(BF16), (named[0] + named[1]).astype(BF16))
+    tables = []
+    for k in range(2):
+        slot = jnp.sum(earlier * named[k], axis=1, keepdims=True)
+        target = picks[k].astype(F32) * CAP + slot
+        tables.append(jnp.where(lane.astype(F32) == target, 1.0, 0.0))
+    dispatch_t = (tables[0] + tables[1]).T.astype(BF16)
+    combine = jnp.concatenate(tables, 0).astype(BF16)
+
+    for half in range(2):
+        keeper = core if half else 1 - core
+        for z in range(chips):
+            start = pl.multiple_of((2 * z + keeper) * rows, rows)
+            q_sorted[pl.ds((half * chips + z) * rows, rows), :] = q_ref[pl.ds(start, rows), :]
+
+    scale = HEAD_DIM ** (-0.5)
+    head_count = q_ref.shape[1] // HEAD_DIM
+    contract = (((1,), (1,)), ((), ()))
+
+    def scores_of(half, h, keys):
+        cols = pl.ds(h * HEAD_DIM, HEAD_DIM)
+        return (
+            lax.dot_general(
+                q_sorted[pl.ds(half * group_rows, group_rows), cols],
+                keys[:, cols],
+                contract,
+                preferred_element_type=F32,
+            )
+            * scale
+        )
+
+    def attend(half):
+        for h in range(head_count):
+            cols = pl.ds(h * HEAD_DIM, HEAD_DIM)
+            near, far = scores_of(half, h, k_ref), scores_of(half, h, k_other)
+            top = jnp.maximum(
+                jnp.max(near, axis=1, keepdims=True), jnp.max(far, axis=1, keepdims=True)
+            )
+            near, far = jnp.exp(near - top), jnp.exp(far - top)
+            total = jnp.sum(near, axis=1, keepdims=True) + jnp.sum(far, axis=1, keepdims=True)
+            numerator = dot(near.astype(BF16), v_ref[:, cols]) + dot(
+                far.astype(BF16), v_other[:, cols]
+            )
+            attn[:, cols] = (numerator / total).astype(BF16)
+
+    k_copy.wait_recv()
+    v_copy.wait_recv()
+    mate = {"ctx": ctx, "exp": exp + 1 - 2 * core}
+    attend(0)
+    loads[0].wait()
+    mate_out[...] = dot(attn[...], wo[...]).astype(BF16)
+    mate_copy = remote(mate_out, mate_in, mate_send, mate_recv, mate)
+    attend(1)
+    own_part[...] = dot(attn[...], wo[...])
+    mate_copy.wait_recv()
+    red_copies = []
+    for dz in range(chips - 1, 0, -1):
+        to_chip = lax.rem(chip + dz, chips)
+        start = pl.multiple_of(to_chip * rows, rows)
+        reduce_out[dz - 1] = (
+            own_part[pl.ds(start, rows), :] + mate_in[pl.ds(start, rows), :].astype(F32)
+        ).astype(BF16)
+        red_copies.append(
+            remote(
+                reduce_out.at[dz - 1],
+                reduce_in.at[dz - 1],
+                red_send.at[dz - 1],
+                red_recv.at[dz - 1],
+                {"ctx": ctx, "exp": 2 * to_chip + core},
+            )
+        )
+    start = pl.multiple_of(chip * rows, rows)
+    hidden[...] = (
+        res_ref[...].astype(F32)
+        + own_part[pl.ds(start, rows), :]
+        + mate_in[pl.ds(start, rows), :].astype(F32)
+    )
+    for dz, copy in zip(range(chips - 1, 0, -1), red_copies):
+        copy.wait_recv()
+        hidden[...] += reduce_in[dz - 1].astype(F32)
+
+    square = jnp.mean(hidden[...] * hidden[...], axis=1, keepdims=True)
+    normed = (hidden[...] * lax.rsqrt(square + 1e-06)).astype(BF16)
+    for c in range(2):
+        sent = dot(dispatch_t, normed[:, c * HALF : (c + 1) * HALF]).astype(BF16)
+        outgoing[c] = sent.reshape(owners, CAP, HALF)
+    disp_copies = {}
+    order = sorted(partners, key=lambda p: (-p[0], abs(p[1] - owners // 2)))
+    for dc, de in order:
+        disp_copies[dc, de] = remote(
+            outgoing.at[other_ctx if dc else ctx, de],
+            slab.at[dc, de],
+            disp_send.at[dc, de],
+            disp_recv.at[dc, de],
+            place(dc, de),
+        )
+    slab[0, 0] = outgoing[ctx, 0]
+    for de in range(owners):
+        disp_copies[1, de].wait_recv()
+    loads[1].wait()
+    loads[2].wait()
+    far_rows = slab[1].reshape(slots, HALF)
+    part_copies = []
+    for n, weight in enumerate((wg, wu)):
+        part_out[n] = dot(far_rows, weight[...]).astype(BF16)
+        part_copies.append(
+            remote(part_out.at[n], part_in.at[n], part_send.at[n], part_recv.at[n], across)
+        )
+    for de in range(1, owners):
+        disp_copies[0, de].wait_recv()
+    near_rows = slab[0].reshape(slots, HALF)
+    gate_part = dot(near_rows, wg[...])
+    up_part = dot(near_rows, wu[...])
+    part_copies[0].wait_recv()
+    gate_part = gate_part + part_in[0].astype(F32)
+    gate_part = gate_part / (1.0 + jnp.exp(-gate_part))
+    part_copies[1].wait_recv()
+    act_own[...] = (gate_part * (up_part + part_in[1].astype(F32))).astype(BF16)
+    act_copy = remote(act_own, act_other, act_send, act_recv, across)
+    loads[3].wait()
+    ret_copies = {}
+    for dc in range(2):
+        if dc:
+            act_copy.wait_recv()
+        result = dot((act_other if dc else act_own)[...], wd[...]).astype(BF16)
+        results[dc] = result.reshape(owners, CAP, HALF)
+        for de in sorted(range(owners), key=lambda e: abs(e - owners // 2)):
+            if dc or de:
+                ret_copies[dc, de] = remote(
+                    results.at[dc, de],
+                    returned.at[dc, de],
+                    ret_send.at[dc, de],
+                    ret_recv.at[dc, de],
+                    place(dc, owners - de if de else 0),
+                )
+    returned[0, 0] = results[0, 0]
+    for dc in range(2):
+        for de in range(owners):
+            if dc or de:
+                ret_copies[dc, de].wait_recv()
+        per_route = dot(combine, returned[dc].reshape(slots, HALF))
+        cols = pl.ds(pl.multiple_of((other_ctx if dc else ctx) * HALF, HALF), HALF)
+        out_ref[:, cols] = (
+            hidden[:, cols]
+            + per_route[:rows] * gates_ref[:, 0:1]
+            + per_route[rows:] * gates_ref[:, 1:2]
+        ).astype(BF16)
+
+    for copy in (
+        [k_copy, v_copy, mate_copy, act_copy]
+        + red_copies
+        + part_copies
+        + list(disp_copies.values())
+        + list(ret_copies.values())
+    ):
+        copy.wait_send()
+
+
+def per_device_pair(
+    owners,
+    queries,
+    keys,
+    values,
+    out_weight,
+    residual_in,
+    gate_weight,
+    up_weight,
+    down_weight,
+    expert_ids,
+    route_gates,
+):
+    tokens, width = queries.shape
+    rows = residual_in.shape[0]
+    units = gate_weight.shape[2]
+    chips, slots = owners // 2, owners * CAP
+    in_vmem = pl.BlockSpec(memory_space=pltpu.VMEM)
+    anywhere = pl.BlockSpec(memory_space=pl.ANY)
+    dma = pltpu.SemaphoreType.DMA
+    return pl.pallas_call(
+        functools.partial(block_kernel, owners),
+        out_shape=jax.ShapeDtypeStruct((rows, D), BF16),
+        in_specs=[in_vmem] * 3
+        + [anywhere, in_vmem, anywhere, anywhere, anywhere, in_vmem, in_vmem],
+        out_specs=in_vmem,
+        scratch_shapes=[
+            pltpu.VMEM((width, D), BF16),
+            pltpu.VMEM((HALF, units), BF16),
+            pltpu.VMEM((HALF, units), BF16),
+            pltpu.VMEM((units, HALF), BF16),
+            pltpu.VMEM((tokens, width), BF16),
+            pltpu.VMEM((tokens, width), BF16),
+            pltpu.VMEM((tokens, width), BF16),
+            pltpu.VMEM((chips * rows, width), BF16),
+            pltpu.VMEM((chips * rows, D), BF16),
+            pltpu.VMEM((chips * rows, D), BF16),
+            pltpu.VMEM((chips * rows, D), F32),
+            pltpu.VMEM((chips - 1, rows, D), BF16),
+            pltpu.VMEM((chips - 1, rows, D), BF16),
+            pltpu.VMEM((rows, D), F32),
+            pltpu.VMEM((2, owners, CAP, HALF), BF16),
+            pltpu.VMEM((2, owners, CAP, HALF), BF16),
+            pltpu.VMEM((2, slots, units), BF16),
+            pltpu.VMEM((2, slots, units), BF16),
+            pltpu.VMEM((slots, units), BF16),
+            pltpu.VMEM((slots, units), BF16),
+            pltpu.VMEM((2, owners, CAP, HALF), BF16),
+            pltpu.VMEM((2, owners, CAP, HALF), BF16),
+            dma((4,)),
+            dma((2,)),
+            dma((2,)),
+            dma,
+            dma,
+            dma((chips - 1,)),
+            dma((chips - 1,)),
+            dma((2, owners)),
+            dma((2, owners)),
+            dma((2,)),
+            dma((2,)),
+            dma,
+            dma,
+            dma((2, owners)),
+            dma((2, owners)),
+        ],
+        compiler_params=pltpu.CompilerParams(
+            collective_id=0, has_side_effects=True, vmem_limit_bytes=40 * 1024 * 1024
+        ),
+    )(
+        queries,
+        keys,
+        values,
+        out_weight,
+        residual_in,
+        gate_weight[0],
+        up_weight[0],
+        down_weight[0],
+        expert_ids,
+        route_gates,
+    )
+
+
 def solution(mesh):
+    if mesh.shape["ctx"] == 2 and mesh.shape["exp"] % 2 == 0:
+        body = functools.partial(per_device_pair, mesh.shape["exp"])
+    else:
+        body = per_device
     return jax.shard_map(
-        per_device,
+        body,
         mesh=mesh,
         in_specs=(
             P(("group", "ctx"), "exp"),

time: 192 us -> 73.4 us (0.38)
  the two profiles are of different devices: /device:TPU:3 before, /device:TPU:0 now
where the time goes in v2:
time: 73.4 us; the launch traced here: 73.1 us
  Pallas kernels  62.6 us (85%)
  local copies, waits for them, and re-layouts  10.4 us (14%)
    pallas_call x1, Pallas kernels, per_device_pair(): pl.pallas_call(functools.partial(block_kernel, owners), out_shape=jax.Sha...  62.6 us
    unnamed x19, local copies, waits for them, and re-layouts  10.4 us

profile of v2, /device:TPU:0, one launch (start us, length us, event | category | flops | bytes accessed | tf_op | source)
XLA Modules:
  0.0 73.1 jit_solution(17173818131227507420)
XLA Ops:
  0.0 0.8 %copy.13.ids_ref = s32[32,2]{1,0:T(8,128)S(1)} copy(s32[32,2]{0,1:T(2,128)} %param.18) | data formatting | bytes 512 | tf_op args[8]
  0.8 1.4 %copy.14.gates_ref = f32[32,2]{1,0:T(8,128)} copy(f32[32,2]{0,1:T(2,128)} %param.19) | data formatting | bytes 512 | tf_op args[9]
  2.1 1.7 %copy.11 = bf16[1,1024,704]{2,1,0:T(8,128)(2,1)S(1)} copy(bf16[1,1024,704]{1,2,0:T(8,128)(2,1)} %param.15) | data formatting | bytes 2883584 | tf_op args[5]
  3.8 0.0 copy-start.2
  3.8 0.0 copy-start.3
  3.8 0.0 copy-start.4
  3.9 1.7 %copy.12 = bf16[1,1024,704]{2,1,0:T(8,128)(2,1)S(1)} copy(bf16[1,1024,704]{1,2,0:T(8,128)(2,1)} %param.16) | data formatting | bytes 2883584 | tf_op args[6]
  5.6 0.0 copy-done.2
  5.6 0.0 copy-done.3
  5.6 0.0 copy-done.4
  5.6 0.0 copy-start
  5.6 1.4 %copy-done = bf16[1,704,1024]{2,1,0:T(8,128)(2,1)S(1)} copy-done((bf16[1,704,1024]{2,1,0:T(8,128)(2,1)S(1)}, bf16[1,704,1024]{2,1,0:T(8,128)(2,1)}, u32[]{:S(2)}) %copy-start) | copy-done | bytes 1441816
  7.0 0.0 copy-start.1
  7.0 1.2 %copy-done.1 = bf16[256,2048]{1,0:T(8,128)(2,1)S(1)} copy-done((bf16[256,2048]{1,0:T(8,128)(2,1)S(1)}, bf16[256,2048]{1,0:T(8,128)(2,1)}, u32[]{:S(2)}) %copy-start.1) | copy-done | bytes 1048600
  8.2 0.0 copy-start.5
  8.2 0.9 %copy-done.5 = bf16[32,2048]{1,0:T(8,128)(2,1)S(1)} copy-done((bf16[32,2048]{1,0:T(8,128)(2,1)S(1)}, bf16[32,2048]{1,0:T(8,128)(2,1)}, u32[]{:S(2)}) %copy-start.5) | copy-done | bytes 131096
  9.1 0.0 copy-start.6
  9.1 0.7 copy-done.6
  9.8 62.6 %shard_map.100 = bf16[32,2048]{1,0:T(8,128)(2,1)S(1)} custom-call(bf16[256,256]{1,0:T(8,128)(2,1)S(1)} %copy-done.2, bf16[256,256]{1,0:T(8,128)(2,1)S(1)} %copy-done.3, bf16[256,256]{1,0:T(8,128)(2,1)S(1)} %copy-done.4, bf16[256,2048]{1,0:T(8,128)(2,1)S(1)} %copy-done.1, bf16[32,2048]{1,0:T(8,128)(2,1)S(1)} %copy-done.5, bf16[1024,704]{1,0:T(8,128)(2,1)S(1)} %bitcast.3, ...), custom_call_target="tpu_custom_call" | custom-call | tf_op jit(solution)/shard_map/pallas_call | solution.py:405
  72.4 0.7 copy.16
Async XLA Ops:
  3.8 1.8 %copy-start.2 = (bf16[256,256]{1,0:T(8,128)(2,1)S(1)}, bf16[256,256]{1,0:T(8,128)(2,1)}, u32[]{:S(2)}) copy-start(bf16[256,256]{1,0:T(8,128)(2,1)} %q_ref.1) | copy-start | bytes 393220
  3.8 1.8 %copy-start.3 = (bf16[256,256]{1,0:T(8,128)(2,1)S(1)}, bf16[256,256]{1,0:T(8,128)(2,1)}, u32[]{:S(2)}) copy-start(bf16[256,256]{1,0:T(8,128)(2,1)} %k_ref.1) | copy-start | bytes 393220
  3.8 1.8 %copy-start.4 = (bf16[256,256]{1,0:T(8,128)(2,1)S(1)}, bf16[256,256]{1,0:T(8,128)(2,1)}, u32[]{:S(2)}) copy-start(bf16[256,256]{1,0:T(8,128)(2,1)} %v_ref.1) | copy-start | bytes 393220
  5.6 1.4 %copy-start = (bf16[1,704,1024]{2,1,0:T(8,128)(2,1)S(1)}, bf16[1,704,1024]{2,1,0:T(8,128)(2,1)}, u32[]{:S(2)}) copy-start(bf16[1,704,1024]{2,1,0:T(8,128)(2,1)} %param.17) | copy-start | bytes 4325380
  7.0 1.2 %copy-start.1 = (bf16[256,2048]{1,0:T(8,128)(2,1)S(1)}, bf16[256,2048]{1,0:T(8,128)(2,1)}, u32[]{:S(2)}) copy-start(bf16[256,2048]{1,0:T(8,128)(2,1)} %wo_hbm.1) | copy-start | bytes 3145732
  8.2 0.9 %copy-start.5 = (bf16[32,2048]{1,0:T(8,128)(2,1)S(1)}, bf16[32,2048]{1,0:T(8,128)(2,1)}, u32[]{:S(2)}) copy-start(bf16[32,2048]{1,0:T(8,128)(2,1)} %res_ref.1) | copy-start | bytes 393220
  9.1 0.7 copy-start.6

commit v3 on v2

--- a/solution.py
+++ b/solution.py
@@ -118,17 +118,22 @@
 
 def block_kernel(
     owners,
-    q_ref,
-    k_ref,
-    v_ref,
+    q_hbm,
+    k_hbm,
+    v_hbm,
     wo_hbm,
-    res_ref,
+    res_hbm,
     wg_hbm,
     wu_hbm,
     wd_hbm,
+    ids_hbm,
+    gates_hbm,
+    out_ref,
+    k_ref,
+    v_ref,
+    res_ref,
     ids_ref,
     gates_ref,
-    out_ref,
     wo,
     wg,
     wu,
@@ -152,6 +157,7 @@
     results,
     returned,
     load_sem,
+    q_sem,
     kv_send,
     kv_recv,
     mate_send,
@@ -182,6 +188,9 @@
             "exp": lax.rem(exp + de, owners) if de else exp,
         }
 
+    def dot_t(a, b):
+        return lax.dot_general(a, b, (((1,), (1,)), ((), ())), preferred_element_type=F32)
+
     def remote(src, dst, send, recv, where):
         copy = pltpu.make_async_remote_copy(
             src_ref=src,
@@ -194,11 +203,29 @@
         copy.start()
         return copy
 
-    loads = []
-    for n, (src, dst) in enumerate(((wo_hbm, wo), (wg_hbm, wg), (wu_hbm, wu), (wd_hbm, wd))):
-        load = pltpu.make_async_copy(src, dst, load_sem.at[n])
-        load.start()
-        loads.append(load)
+    def load(n, src, dst):
+        copy = pltpu.make_async_copy(src, dst, load_sem.at[n])
+        copy.start()
+        return copy
+
+    q_loads = []
+    for n in range(owners):
+        keeper = core if n >= chips else 1 - core
+        start = pl.multiple_of((2 * (n % chips) + keeper) * rows, rows)
+        copy = pltpu.make_async_copy(
+            q_hbm.at[pl.ds(start, rows), :], q_sorted.at[pl.ds(n * rows, rows), :], q_sem.at[n]
+        )
+        copy.start()
+        q_loads.append(copy)
+    k_load = load(0, k_hbm, k_ref)
+    v_load = load(1, v_hbm, v_ref)
+    ids_load = load(2, ids_hbm, ids_ref)
+    gates_load = load(3, gates_hbm, gates_ref)
+    wo_load = load(4, wo_hbm, wo)
+    res_load = load(5, res_hbm, res_ref)
+    wg_load = load(6, wg_hbm, wg)
+    wu_load = load(7, wu_hbm, wu)
+    wd_load = load(8, wd_hbm, wd)
 
     partners = [(dc, de) for dc in range(2) for de in range(owners) if dc or de]
     barrier = pltpu.get_barrier_semaphore()
@@ -209,38 +236,35 @@
     pl.semaphore_wait(barrier, len(partners))
 
     across = place(1, 0)
-    k_copy = remote(k_ref, k_other, kv_send.at[0], kv_recv.at[0], across)
-    v_copy = remote(v_ref, v_other, kv_send.at[1], kv_recv.at[1], across)
-
-    lane = lax.broadcasted_iota(jnp.int32, (rows, slots), 1)
+    k_copy = remote(k_hbm, k_other, kv_send.at[0], kv_recv.at[0], across)
+    v_copy = remote(v_hbm, v_other, kv_send.at[1], kv_recv.at[1], across)
+
+    ids_load.wait()
+    gates_load.wait()
+    line = lax.broadcasted_iota(jnp.int32, (slots, rows), 0)
     picks = []
     for k in range(2):
-        rel = ids_ref[:, k : k + 1] - exp
+        rel = ids_ref[k : k + 1, :] - exp
         picks.append(jnp.where(rel < 0, rel + owners, rel))
-    named = [jnp.where(lane == rel, 1.0, 0.0) for rel in picks]
-    below = jnp.where(
-        lax.broadcasted_iota(jnp.int32, (rows, rows), 0)
-        > lax.broadcasted_iota(jnp.int32, (rows, rows), 1),
-        1.0,
-        0.0,
-    )
-    earlier = dot(below.astype(BF16), (named[0] + named[1]).astype(BF16))
+    named = [jnp.where(line == rel, 1.0, 0.0) for rel in picks]
+    down_row = lax.broadcasted_iota(jnp.int32, (rows, rows), 0)
+    down_col = lax.broadcasted_iota(jnp.int32, (rows, rows), 1)
+    before = jnp.where(down_row < down_col, 1.0, 0.0)
+    same = jnp.where(down_row == down_col, 1.0, 0.0)
+    earlier = dot((named[0] + named[1]).astype(BF16), before.astype(BF16))
     tables = []
     for k in range(2):
-        slot = jnp.sum(earlier * named[k], axis=1, keepdims=True)
+        slot = jnp.sum(earlier * named[k], axis=0, keepdims=True)
         target = picks[k].astype(F32) * CAP + slot
-        tables.append(jnp.where(lane.astype(F32) == target, 1.0, 0.0))
-    dispatch_t = (tables[0] + tables[1]).T.astype(BF16)
-    combine = jnp.concatenate(tables, 0).astype(BF16)
-
-    for half in range(2):
-        keeper = core if half else 1 - core
-        for z in range(chips):
-            start = pl.multiple_of((2 * z + keeper) * rows, rows)
-            q_sorted[pl.ds((half * chips + z) * rows, rows), :] = q_ref[pl.ds(start, rows), :]
+        tables.append(jnp.where(line.astype(F32) == target, 1.0, 0.0))
+    dispatch_t = (tables[0] + tables[1]).astype(BF16)
+    combine = jnp.concatenate([table.T for table in tables], 0).astype(BF16)
+    gate_columns = [
+        jnp.sum(same * gates_ref[k : k + 1, :], axis=1, keepdims=True) for k in range(2)
+    ]
 
     scale = HEAD_DIM ** (-0.5)
-    head_count = q_ref.shape[1] // HEAD_DIM
+    head_count = q_sorted.shape[1] // HEAD_DIM
     contract = (((1,), (1,)), ((), ()))
 
     def scores_of(half, h, keys):
@@ -255,10 +279,19 @@
             * scale
         )
 
+    for copy in q_loads:
+        copy.wait()
+    k_load.wait()
+    v_load.wait()
+    near_scores = {}
+    for half in range(2):
+        for h in range(head_count):
+            near_scores[half, h] = scores_of(half, h, k_ref)
+
     def attend(half):
         for h in range(head_count):
             cols = pl.ds(h * HEAD_DIM, HEAD_DIM)
-            near, far = scores_of(half, h, k_ref), scores_of(half, h, k_other)
+            near, far = near_scores[half, h], scores_of(half, h, k_other)
             top = jnp.maximum(
                 jnp.max(near, axis=1, keepdims=True), jnp.max(far, axis=1, keepdims=True)
             )
@@ -273,37 +306,46 @@
     v_copy.wait_recv()
     mate = {"ctx": ctx, "exp": exp + 1 - 2 * core}
     attend(0)
-    loads[0].wait()
-    mate_out[...] = dot(attn[...], wo[...]).astype(BF16)
-    mate_copy = remote(mate_out, mate_in, mate_send, mate_recv, mate)
+    wo_load.wait()
+    mate_copies = []
+    for c in range(2):
+        mate_out[c] = dot(attn[...], wo[:, c * HALF : (c + 1) * HALF]).astype(BF16)
+        mate_copies.append(
+            remote(mate_out.at[c], mate_in.at[c], mate_send.at[c], mate_recv.at[c], mate)
+        )
     attend(1)
-    own_part[...] = dot(attn[...], wo[...])
-    mate_copy.wait_recv()
     red_copies = []
-    for dz in range(chips - 1, 0, -1):
-        to_chip = lax.rem(chip + dz, chips)
-        start = pl.multiple_of(to_chip * rows, rows)
-        reduce_out[dz - 1] = (
-            own_part[pl.ds(start, rows), :] + mate_in[pl.ds(start, rows), :].astype(F32)
-        ).astype(BF16)
-        red_copies.append(
-            remote(
-                reduce_out.at[dz - 1],
-                reduce_in.at[dz - 1],
-                red_send.at[dz - 1],
-                red_recv.at[dz - 1],
-                {"ctx": ctx, "exp": 2 * to_chip + core},
+    own_start = pl.multiple_of(chip * rows, rows)
+    res_load.wait()
+    for c in range(2):
+        cols = pl.ds(c * HALF, HALF)
+        own_part[...] = dot(attn[...], wo[:, cols])
+        mate_copies[c].wait_recv()
+        for dz in range(chips - 1, 0, -1):
+            to_chip = lax.rem(chip + dz, chips)
+            start = pl.multiple_of(to_chip * rows, rows)
+            reduce_out[c, dz - 1] = (
+                own_part[pl.ds(start, rows), :] + mate_in[c, pl.ds(start, rows), :].astype(F32)
+            ).astype(BF16)
+            red_copies.append(
+                remote(
+                    reduce_out.at[c, dz - 1],
+                    reduce_in.at[c, dz - 1],
+                    red_send.at[c, dz - 1],
+                    red_recv.at[c, dz - 1],
+                    {"ctx": ctx, "exp": 2 * to_chip + core},
+                )
             )
-        )
-    start = pl.multiple_of(chip * rows, rows)
-    hidden[...] = (
-        res_ref[...].astype(F32)
-        + own_part[pl.ds(start, rows), :]
-        + mate_in[pl.ds(start, rows), :].astype(F32)
-    )
-    for dz, copy in zip(range(chips - 1, 0, -1), red_copies):
-        copy.wait_recv()
-        hidden[...] += reduce_in[dz - 1].astype(F32)
+        hidden[:, cols] = (
+            res_ref[:, cols].astype(F32)
+            + own_part[pl.ds(own_start, rows), :]
+            + mate_in[c, pl.ds(own_start, rows), :].astype(F32)
+        )
+    for c in range(2):
+        cols = pl.ds(c * HALF, HALF)
+        for dz in range(chips - 1, 0, -1):
+            red_copies[c * (chips - 1) + chips - 1 - dz].wait_recv()
+            hidden[:, cols] += reduce_in[c, dz - 1].astype(F32)
 
     square = jnp.mean(hidden[...] * hidden[...], axis=1, keepdims=True)
     normed = (hidden[...] * lax.rsqrt(square + 1e-06)).astype(BF16)
@@ -323,27 +365,27 @@
     slab[0, 0] = outgoing[ctx, 0]
     for de in range(owners):
         disp_copies[1, de].wait_recv()
-    loads[1].wait()
-    loads[2].wait()
+    wg_load.wait()
+    wu_load.wait()
     far_rows = slab[1].reshape(slots, HALF)
     part_copies = []
     for n, weight in enumerate((wg, wu)):
-        part_out[n] = dot(far_rows, weight[...]).astype(BF16)
+        part_out[n] = dot_t(far_rows, weight[...]).astype(BF16)
         part_copies.append(
             remote(part_out.at[n], part_in.at[n], part_send.at[n], part_recv.at[n], across)
         )
     for de in range(1, owners):
         disp_copies[0, de].wait_recv()
     near_rows = slab[0].reshape(slots, HALF)
-    gate_part = dot(near_rows, wg[...])
-    up_part = dot(near_rows, wu[...])
+    gate_part = dot_t(near_rows, wg[...])
+    up_part = dot_t(near_rows, wu[...])
     part_copies[0].wait_recv()
     gate_part = gate_part + part_in[0].astype(F32)
     gate_part = gate_part / (1.0 + jnp.exp(-gate_part))
     part_copies[1].wait_recv()
     act_own[...] = (gate_part * (up_part + part_in[1].astype(F32))).astype(BF16)
     act_copy = remote(act_own, act_other, act_send, act_recv, across)
-    loads[3].wait()
+    wd_load.wait()
     ret_copies = {}
     for dc in range(2):
         if dc:
@@ -368,12 +410,13 @@
         cols = pl.ds(pl.multiple_of((other_ctx if dc else ctx) * HALF, HALF), HALF)
         out_ref[:, cols] = (
             hidden[:, cols]
-            + per_route[:rows] * gates_ref[:, 0:1]
-            + per_route[rows:] * gates_ref[:, 1:2]
+            + per_route[:rows] * gate_columns[0]
+            + per_route[rows:] * gate_columns[1]
         ).astype(BF16)
 
     for copy in (
-        [k_copy, v_copy, mate_copy, act_copy]
+        [k_copy, v_copy, act_copy]
+        + mate_copies
         + red_copies
         + part_copies
         + list(disp_copies.values())
@@ -400,28 +443,31 @@
     units = gate_weight.shape[2]
     chips, slots = owners // 2, owners * CAP
     in_vmem = pl.BlockSpec(memory_space=pltpu.VMEM)
-    anywhere = pl.BlockSpec(memory_space=pl.ANY)
     dma = pltpu.SemaphoreType.DMA
     return pl.pallas_call(
         functools.partial(block_kernel, owners),
         out_shape=jax.ShapeDtypeStruct((rows, D), BF16),
-        in_specs=[in_vmem] * 3
-        + [anywhere, in_vmem, anywhere, anywhere, anywhere, in_vmem, in_vmem],
+        in_specs=[pl.BlockSpec(memory_space=pltpu.HBM)] * 10,
         out_specs=in_vmem,
         scratch_shapes=[
+            pltpu.VMEM((tokens, width), BF16),
+            pltpu.VMEM((tokens, width), BF16),
+            pltpu.VMEM((rows, D), BF16),
+            pltpu.VMEM((2, rows), jnp.int32),
+            pltpu.VMEM((2, rows), F32),
             pltpu.VMEM((width, D), BF16),
-            pltpu.VMEM((HALF, units), BF16),
-            pltpu.VMEM((HALF, units), BF16),
+            pltpu.VMEM((units, HALF), BF16),
+            pltpu.VMEM((units, HALF), BF16),
             pltpu.VMEM((units, HALF), BF16),
             pltpu.VMEM((tokens, width), BF16),
             pltpu.VMEM((tokens, width), BF16),
             pltpu.VMEM((tokens, width), BF16),
             pltpu.VMEM((chips * rows, width), BF16),
-            pltpu.VMEM((chips * rows, D), BF16),
-            pltpu.VMEM((chips * rows, D), BF16),
-            pltpu.VMEM((chips * rows, D), F32),
-            pltpu.VMEM((chips - 1, rows, D), BF16),
-            pltpu.VMEM((chips - 1, rows, D), BF16),
+            pltpu.VMEM((2, chips * rows, HALF), BF16),
+            pltpu.VMEM((2, chips * rows, HALF), BF16),
+            pltpu.VMEM((chips * rows, HALF), F32),
+            pltpu.VMEM((2, chips - 1, rows, HALF), BF16),
+            pltpu.VMEM((2, chips - 1, rows, HALF), BF16),
             pltpu.VMEM((rows, D), F32),
             pltpu.VMEM((2, owners, CAP, HALF), BF16),
             pltpu.VMEM((2, owners, CAP, HALF), BF16),
@@ -431,13 +477,14 @@
             pltpu.VMEM((slots, units), BF16),
             pltpu.VMEM((2, owners, CAP, HALF), BF16),
             pltpu.VMEM((2, owners, CAP, HALF), BF16),
-            dma((4,)),
+            dma((9,)),
+            dma((owners,)),
             dma((2,)),
             dma((2,)),
-            dma,
-            dma,
-            dma((chips - 1,)),
-            dma((chips - 1,)),
+            dma((2,)),
+            dma((2,)),
+            dma((2, chips - 1)),
+            dma((2, chips - 1)),
             dma((2, owners)),
             dma((2, owners)),
             dma((2,)),
@@ -448,7 +495,7 @@
             dma((2, owners)),
         ],
         compiler_params=pltpu.CompilerParams(
-            collective_id=0, has_side_effects=True, vmem_limit_bytes=40 * 1024 * 1024
+            collective_id=0, has_side_effects=True, vmem_limit_bytes=64 * 1024 * 1024
         ),
     )(
         queries,
@@ -456,11 +503,11 @@
         values,
         out_weight,
         residual_in,
-        gate_weight[0],
-        up_weight[0],
+        gate_weight[0].T,
+        up_weight[0].T,
         down_weight[0],
-        expert_ids,
-        route_gates,
+        expert_ids.T,
+        route_gates.T,
     )
 
 

time: 73.4 us -> 67.4 us (0.918)
  the two profiles are of different devices: /device:TPU:0 before, /device:TPU:3 now
where the time goes in v3:
time: 67.4 us; the launch traced here: 67.3 us
  Pallas kernels  65.7 us (97%)
  local copies, waits for them, and re-layouts  1.57 us (2%)
    pallas_call x1, Pallas kernels, per_device_pair(): pl.pallas_call(functools.partial(block_kernel, owners), out_shape=jax.Sha...  65.7 us
    unnamed x1, local copies, waits for them, and re-layouts  1.57 us

profile of v3, /device:TPU:3, one launch (start us, length us, event | category | flops | bytes accessed | tf_op | source)
XLA Modules:
  0.0 67.3 jit_solution(10897711021268686016)
XLA Ops:
  0.0 65.7 %shard_map.100 = bf16[32,2048]{1,0:T(8,128)(2,1)} custom-call(bf16[256,256]{1,0:T(8,128)(2,1)} %q_hbm.1, bf16[256,256]{1,0:T(8,128)(2,1)} %k_hbm.1, bf16[256,256]{1,0:T(8,128)(2,1)} %v_hbm.1, bf16[256,2048]{1,0:T(8,128)(2,1)} %wo_hbm.1, bf16[32,2048]{1,0:T(8,128)(2,1)} %res_hbm.1, bf16[704,1024]{1,0:T(8,128)(2,1)} %bitcast.9, bf16[704,1024]{1,0:T(8,128)(2,1)} %bitcast.10, ...), custom_call_target="tpu_custom_call" | custom-call | tf_op jit(solution)/shard_map/pallas_call | solution.py:447
  65.7 1.6 %copy.12 = bf16[32,2048]{1,0:T(8,128)(2,1)} copy(bf16[32,2048]{1,0:T(8,128)(2,1)} %shard_map.100) | data formatting | bytes 262144

commit v4 on v3

--- a/solution.py
+++ b/solution.py
@@ -265,61 +265,46 @@
 
     scale = HEAD_DIM ** (-0.5)
     head_count = q_sorted.shape[1] // HEAD_DIM
-    contract = (((1,), (1,)), ((), ()))
-
-    def scores_of(half, h, keys):
+
+    def scores_of(h, keys):
         cols = pl.ds(h * HEAD_DIM, HEAD_DIM)
-        return (
-            lax.dot_general(
-                q_sorted[pl.ds(half * group_rows, group_rows), cols],
-                keys[:, cols],
-                contract,
-                preferred_element_type=F32,
-            )
-            * scale
-        )
+        return dot_t(q_sorted[:, cols], keys[:, cols]) * scale
 
     for copy in q_loads:
         copy.wait()
     k_load.wait()
     v_load.wait()
-    near_scores = {}
-    for half in range(2):
-        for h in range(head_count):
-            near_scores[half, h] = scores_of(half, h, k_ref)
-
-    def attend(half):
-        for h in range(head_count):
-            cols = pl.ds(h * HEAD_DIM, HEAD_DIM)
-            near, far = near_scores[half, h], scores_of(half, h, k_other)
-            top = jnp.maximum(
-                jnp.max(near, axis=1, keepdims=True), jnp.max(far, axis=1, keepdims=True)
-            )
-            near, far = jnp.exp(near - top), jnp.exp(far - top)
-            total = jnp.sum(near, axis=1, keepdims=True) + jnp.sum(far, axis=1, keepdims=True)
-            numerator = dot(near.astype(BF16), v_ref[:, cols]) + dot(
-                far.astype(BF16), v_other[:, cols]
-            )
-            attn[:, cols] = (numerator / total).astype(BF16)
-
+    wo_load.wait()
+    near_scores = [scores_of(h, k_ref) for h in range(head_count)]
+    near_tops = [jnp.max(near, axis=1, keepdims=True) for near in near_scores]
     k_copy.wait_recv()
+    softmax = []
+    for h in range(head_count):
+        far = scores_of(h, k_other)
+        top = jnp.maximum(near_tops[h], jnp.max(far, axis=1, keepdims=True))
+        near, far = jnp.exp(near_scores[h] - top), jnp.exp(far - top)
+        total = jnp.sum(near, axis=1, keepdims=True) + jnp.sum(far, axis=1, keepdims=True)
+        cols = pl.ds(h * HEAD_DIM, HEAD_DIM)
+        softmax.append((dot(near.astype(BF16), v_ref[:, cols]), far.astype(BF16), total))
     v_copy.wait_recv()
+    for h in range(head_count):
+        cols = pl.ds(h * HEAD_DIM, HEAD_DIM)
+        numerator, far, total = softmax[h]
+        attn[:, cols] = ((numerator + dot(far, v_other[:, cols])) / total).astype(BF16)
+
     mate = {"ctx": ctx, "exp": exp + 1 - 2 * core}
-    attend(0)
-    wo_load.wait()
     mate_copies = []
     for c in range(2):
-        mate_out[c] = dot(attn[...], wo[:, c * HALF : (c + 1) * HALF]).astype(BF16)
+        mate_out[c] = dot(attn[:group_rows, :], wo[:, c * HALF : (c + 1) * HALF]).astype(BF16)
         mate_copies.append(
             remote(mate_out.at[c], mate_in.at[c], mate_send.at[c], mate_recv.at[c], mate)
         )
-    attend(1)
     red_copies = []
     own_start = pl.multiple_of(chip * rows, rows)
     res_load.wait()
     for c in range(2):
         cols = pl.ds(c * HALF, HALF)
-        own_part[...] = dot(attn[...], wo[:, cols])
+        own_part[...] = dot(attn[group_rows:, :], wo[:, cols])
         mate_copies[c].wait_recv()
         for dz in range(chips - 1, 0, -1):
             to_chip = lax.rem(chip + dz, chips)
@@ -462,7 +447,7 @@
             pltpu.VMEM((tokens, width), BF16),
             pltpu.VMEM((tokens, width), BF16),
             pltpu.VMEM((tokens, width), BF16),
-            pltpu.VMEM((chips * rows, width), BF16),
+            pltpu.VMEM((tokens, width), BF16),
             pltpu.VMEM((2, chips * rows, HALF), BF16),
             pltpu.VMEM((2, chips * rows, HALF), BF16),
             pltpu.VMEM((chips * rows, HALF), F32),

time: 67.4 us -> 67.1 us (level)
  no operation moved by 1% of the time
where the time goes in v4:
time: 67.1 us; the launch traced here: 66.9 us
  Pallas kernels  65.3 us (97%)
  local copies, waits for them, and re-layouts  1.57 us (2%)
    pallas_call x1, Pallas kernels, per_device_pair(): pl.pallas_call(functools.partial(block_kernel, owners), out_shape=jax.Sha...  65.3 us
    unnamed x1, local copies, waits for them, and re-layouts  1.57 us

profile of v4, /device:TPU:3, one launch (start us, length us, event | category | flops | bytes accessed | tf_op | source)
XLA Modules:
  0.0 66.9 jit_solution(2408887235317621371)
XLA Ops:
  0.0 65.3 %shard_map.100 = bf16[32,2048]{1,0:T(8,128)(2,1)} custom-call(bf16[256,256]{1,0:T(8,128)(2,1)} %q_hbm.1, bf16[256,256]{1,0:T(8,128)(2,1)} %k_hbm.1, bf16[256,256]{1,0:T(8,128)(2,1)} %v_hbm.1, bf16[256,2048]{1,0:T(8,128)(2,1)} %wo_hbm.1, bf16[32,2048]{1,0:T(8,128)(2,1)} %res_hbm.1, bf16[704,1024]{1,0:T(8,128)(2,1)} %bitcast.9, bf16[704,1024]{1,0:T(8,128)(2,1)} %bitcast.10, ...), custom_call_target="tpu_custom_call" | custom-call | tf_op jit(solution)/shard_map/pallas_call | solution.py:432
  65.4 1.6 %copy.12 = bf16[32,2048]{1,0:T(8,128)(2,1)} copy(bf16[32,2048]{1,0:T(8,128)(2,1)} %shard_map.100) | data formatting | bytes 262144

commit v5 on v4

--- a/solution.py
+++ b/solution.py
@@ -148,6 +148,7 @@
     reduce_out,
     reduce_in,
     hidden,
+    normed_halves,
     outgoing,
     slab,
     part_out,
@@ -328,26 +329,31 @@
         )
     for c in range(2):
         cols = pl.ds(c * HALF, HALF)
+        for copy in red_copies[c * (chips - 1) : (c + 1) * (chips - 1)]:
+            copy.wait_recv()
+        total = hidden[:, cols]
         for dz in range(chips - 1, 0, -1):
-            red_copies[c * (chips - 1) + chips - 1 - dz].wait_recv()
-            hidden[:, cols] += reduce_in[c, dz - 1].astype(F32)
+            total = total + reduce_in[c, dz - 1].astype(F32)
+        hidden[:, cols] = total
 
     square = jnp.mean(hidden[...] * hidden[...], axis=1, keepdims=True)
     normed = (hidden[...] * lax.rsqrt(square + 1e-06)).astype(BF16)
     for c in range(2):
-        sent = dot(dispatch_t, normed[:, c * HALF : (c + 1) * HALF]).astype(BF16)
-        outgoing[c] = sent.reshape(owners, CAP, HALF)
+        normed_halves[c] = normed[:, c * HALF : (c + 1) * HALF]
     disp_copies = {}
-    order = sorted(partners, key=lambda p: (-p[0], abs(p[1] - owners // 2)))
-    for dc, de in order:
-        disp_copies[dc, de] = remote(
-            outgoing.at[other_ctx if dc else ctx, de],
-            slab.at[dc, de],
-            disp_send.at[dc, de],
-            disp_recv.at[dc, de],
-            place(dc, de),
-        )
-    slab[0, 0] = outgoing[ctx, 0]
+    for dc in (1, 0):
+        c = other_ctx if dc else ctx
+        outgoing[dc] = dot(dispatch_t, normed_halves[c]).astype(BF16).reshape(owners, CAP, HALF)
+        for de in sorted(range(owners), key=lambda e: abs(e - owners // 2)):
+            if dc or de:
+                disp_copies[dc, de] = remote(
+                    outgoing.at[dc, de],
+                    slab.at[dc, de],
+                    disp_send.at[dc, de],
+                    disp_recv.at[dc, de],
+                    place(dc, de),
+                )
+    slab[0, 0] = outgoing[0, 0]
     for de in range(owners):
         disp_copies[1, de].wait_recv()
     wg_load.wait()
@@ -454,6 +460,7 @@
             pltpu.VMEM((2, chips - 1, rows, HALF), BF16),
             pltpu.VMEM((2, chips - 1, rows, HALF), BF16),
             pltpu.VMEM((rows, D), F32),
+            pltpu.VMEM((2, rows, HALF), BF16),
             pltpu.VMEM((2, owners, CAP, HALF), BF16),
             pltpu.VMEM((2, owners, CAP, HALF), BF16),
             pltpu.VMEM((2, slots, units), BF16),

time: 67.1 us -> 67 us (level)
  no operation moved by 1% of the time
where the time goes in v5:
time: 67 us; the launch traced here: 66.8 us
  Pallas kernels  65.2 us (97%)
  local copies, waits for them, and re-layouts  1.57 us (2%)
    pallas_call x1, Pallas kernels, per_device_pair(): pl.pallas_call(functools.partial(block_kernel, owners), out_shape=jax.Sha...  65.2 us
    unnamed x1, local copies, waits for them, and re-layouts  1.57 us

profile of v5, /device:TPU:3, one launch (start us, length us, event | category | flops | bytes accessed | tf_op | source)
XLA Modules:
  0.0 66.8 jit_solution(2333354332976885750)
XLA Ops:
  0.0 65.2 %shard_map.100 = bf16[32,2048]{1,0:T(8,128)(2,1)} custom-call(bf16[256,256]{1,0:T(8,128)(2,1)} %q_hbm.1, bf16[256,256]{1,0:T(8,128)(2,1)} %k_hbm.1, bf16[256,256]{1,0:T(8,128)(2,1)} %v_hbm.1, bf16[256,2048]{1,0:T(8,128)(2,1)} %wo_hbm.1, bf16[32,2048]{1,0:T(8,128)(2,1)} %res_hbm.1, bf16[704,1024]{1,0:T(8,128)(2,1)} %bitcast.9, bf16[704,1024]{1,0:T(8,128)(2,1)} %bitcast.10, ...), custom_call_target="tpu_custom_call" | custom-call | tf_op jit(solution)/shard_map/pallas_call | solution.py:438
  65.2 1.6 %copy.12 = bf16[32,2048]{1,0:T(8,128)(2,1)} copy(bf16[32,2048]{1,0:T(8,128)(2,1)} %shard_map.100) | data formatting | bytes 262144

commit v6 on v5

--- a/solution.py
+++ b/solution.py
@@ -238,7 +238,6 @@
 
     across = place(1, 0)
     k_copy = remote(k_hbm, k_other, kv_send.at[0], kv_recv.at[0], across)
-    v_copy = remote(v_hbm, v_other, kv_send.at[1], kv_recv.at[1], across)
 
     ids_load.wait()
     gates_load.wait()
@@ -263,6 +262,8 @@
     gate_columns = [
         jnp.sum(same * gates_ref[k : k + 1, :], axis=1, keepdims=True) for k in range(2)
     ]
+
+    v_copy = remote(v_hbm, v_other, kv_send.at[1], kv_recv.at[1], across)
 
     scale = HEAD_DIM ** (-0.5)
     head_count = q_sorted.shape[1] // HEAD_DIM

time: 67 us -> 67 us (level)
  no operation moved by 1% of the time
where the time goes in v6:
time: 67 us; the launch traced here: 66.9 us
  Pallas kernels  65.3 us (97%)
  local copies, waits for them, and re-layouts  1.57 us (2%)
    pallas_call x1, Pallas kernels, per_device_pair(): pl.pallas_call(functools.partial(block_kernel, owners), out_shape=jax.Sha...  65.3 us
    unnamed x1, local copies, waits for them, and re-layouts  1.57 us

profile of v6, /device:TPU:3, one launch (start us, length us, event | category | flops | bytes accessed | tf_op | source)
XLA Modules:
  0.0 66.9 jit_solution(8342234646459415566)
XLA Ops:
  0.0 65.3 %shard_map.100 = bf16[32,2048]{1,0:T(8,128)(2,1)} custom-call(bf16[256,256]{1,0:T(8,128)(2,1)} %q_hbm.1, bf16[256,256]{1,0:T(8,128)(2,1)} %k_hbm.1, bf16[256,256]{1,0:T(8,128)(2,1)} %v_hbm.1, bf16[256,2048]{1,0:T(8,128)(2,1)} %wo_hbm.1, bf16[32,2048]{1,0:T(8,128)(2,1)} %res_hbm.1, bf16[704,1024]{1,0:T(8,128)(2,1)} %bitcast.9, bf16[704,1024]{1,0:T(8,128)(2,1)} %bitcast.10, ...), custom_call_target="tpu_custom_call" | custom-call | tf_op jit(solution)/shard_map/pallas_call | solution.py:439
  65.3 1.6 %copy.12 = bf16[32,2048]{1,0:T(8,128)(2,1)} copy(bf16[32,2048]{1,0:T(8,128)(2,1)} %shard_map.100) | data formatting | bytes 262144

commit v7 on v5

--- a/solution.py
+++ b/solution.py
@@ -224,10 +224,6 @@
     gates_load = load(3, gates_hbm, gates_ref)
     wo_load = load(4, wo_hbm, wo)
     res_load = load(5, res_hbm, res_ref)
-    wg_load = load(6, wg_hbm, wg)
-    wu_load = load(7, wu_hbm, wu)
-    wd_load = load(8, wd_hbm, wd)
-
     partners = [(dc, de) for dc in range(2) for de in range(owners) if dc or de]
     barrier = pltpu.get_barrier_semaphore()
     for dc, de in partners:
@@ -239,6 +235,9 @@
     across = place(1, 0)
     k_copy = remote(k_hbm, k_other, kv_send.at[0], kv_recv.at[0], across)
     v_copy = remote(v_hbm, v_other, kv_send.at[1], kv_recv.at[1], across)
+    wg_load = load(6, wg_hbm, wg)
+    wu_load = load(7, wu_hbm, wu)
+    wd_load = load(8, wd_hbm, wd)
 
     ids_load.wait()
     gates_load.wait()

time: 67 us -> 67 us (level)
  no operation moved by 1% of the time
where the time goes in v7:
time: 67 us; the launch traced here: 66.8 us
  Pallas kernels  65.3 us (97%)
  local copies, waits for them, and re-layouts  1.57 us (2%)
    pallas_call x1, Pallas kernels, per_device_pair(): pl.pallas_call(functools.partial(block_kernel, owners), out_shape=jax.Sha...  65.3 us
    unnamed x1, local copies, waits for them, and re-layouts  1.57 us

profile of v7, /device:TPU:3, one launch (start us, length us, event | category | flops | bytes accessed | tf_op | source)
XLA Modules:
  0.0 66.8 jit_solution(14713994112586493305)
XLA Ops:
  0.0 65.3 %shard_map.100 = bf16[32,2048]{1,0:T(8,128)(2,1)} custom-call(bf16[256,256]{1,0:T(8,128)(2,1)} %q_hbm.1, bf16[256,256]{1,0:T(8,128)(2,1)} %k_hbm.1, bf16[256,256]{1,0:T(8,128)(2,1)} %v_hbm.1, bf16[256,2048]{1,0:T(8,128)(2,1)} %wo_hbm.1, bf16[32,2048]{1,0:T(8,128)(2,1)} %res_hbm.1, bf16[704,1024]{1,0:T(8,128)(2,1)} %bitcast.9, bf16[704,1024]{1,0:T(8,128)(2,1)} %bitcast.10, ...), custom_call_target="tpu_custom_call" | custom-call | tf_op jit(solution)/shard_map/pallas_call | solution.py:437
  65.3 1.6 %copy.12 = bf16[32,2048]{1,0:T(8,128)(2,1)} copy(bf16[32,2048]{1,0:T(8,128)(2,1)} %shard_map.100) | data formatting | bytes 262144
